TPU v7x, 128 devices: a whole 4x4x4 slice. The times are simulated.
128 devices in a mesh: chan: 32 (over x_hi, z, y), seg: 4 (over x_lo, core).
Axes of the slice: x: 4 (x_hi: 2, x_lo: 2; x = x_hi * 2 + x_lo), y: 4, z: 4, core: 2. Of those that a mesh axis runs over, the one named last changes fastest.
Arguments:
- spectra: bfloat16 [2, 16, 768, 4096], P(None, 'seg', None, 'chan'), may hold values from -50 to 50
- half_width: int32 [768], replicated, may hold values from 2 to 16
- band: int32 [32], replicated, may hold values from 0 to 2, as said below
Outputs:
- correlations: float32 [4096, 3, 128, 256], P(('chan', 'seg'))
Inputs may be any that keep to these rules, and one draw needn't show every extreme that they name: band[0] = 2, band[29] = 2, band[30] >= 1.
All inputs are finite; a program needn't handle non-finite values.
Results may differ from a plain program's by a relative error of at most 0.0046.
Values may be sent and summed in bfloat16 or wider, within the bound.
A program may use at most 192 MiB of HBM per device.

v0:
```python
from functools import partial
import math

import jax
import jax.numpy as jnp
from jax import lax
from jax.sharding import PartitionSpec as P

FLO = 25
NT = 3000
LAGS = 256


floor_value = 0.2
reach = 16


def shifted(array, axis, by):
    size = lax.axis_size(axis)
    pairs = [(i, i + by) for i in range(size) if 0 <= i + by < size]
    return lax.ppermute(array, axis, pairs)


def smooth_bands(amplitude, half_width):
    bins = half_width.shape[0]
    step = min(128, bins)
    index = jnp.arange(bins, dtype=jnp.int32)
    lower = jnp.maximum(index - half_width, 0)
    upper = jnp.minimum(index + half_width, bins - 1)
    count = (upper - lower + 1).astype(jnp.float32)
    padded = jnp.pad(amplitude, ((0, 0), (reach, reach), (0, 0)))
    pieces = []
    for start in range(0, bins, step):
        low_rows = lower[start : start + step]
        high_rows = upper[start : start + step]
        columns = jnp.arange(step + 2 * reach, dtype=jnp.int32) + (start - reach)
        inside = (columns[None, :] >= low_rows[:, None]) & (columns[None, :] <= high_rows[:, None])
        weights = (
            jnp.where(inside, 1.0, 0.0).astype(jnp.float32) / count[start : start + step][:, None]
        )
        window = padded[:, start : start + step + 2 * reach, :]
        pieces.append(jnp.einsum("kj,sjc->skc", weights, window, precision=lax.Precision.HIGHEST))
    return jnp.concatenate(pieces, axis=1)


def whiten(block, half_width):
    real_part = block[0].astype(jnp.float32)
    imag_part = block[1].astype(jnp.float32)
    amplitude = jnp.sqrt(real_part * real_part + imag_part * imag_part)
    smooth = smooth_bands(amplitude, half_width)
    denom = jnp.maximum(smooth, floor_value)
    return jnp.stack([real_part / denom, imag_part / denom]).astype(jnp.bfloat16)


def lag_table(bins, lags):
    index = jnp.arange(bins, dtype=jnp.int32)
    shifts = jnp.arange(lags, dtype=jnp.int32) - lags // 2 + 1
    phase = (FLO + index)[:, None] * shifts[None, :] % NT
    angle = 2.0 * math.pi / NT * phase.astype(jnp.float32)
    return jnp.concatenate([jnp.cos(angle), -jnp.sin(angle)], axis=0).astype(jnp.bfloat16)


def cross_lags(rows, partner, table, norm):
    left_re = jnp.concatenate([rows[0], rows[1]], axis=0)
    left_im = jnp.concatenate([rows[1], -rows[0]], axis=0)
    right = jnp.concatenate([partner[0], partner[1]], axis=0)
    cross_re = jnp.einsum("ska,skb->kab", left_re, right, preferred_element_type=jnp.float32)
    cross_im = jnp.einsum("ska,skb->kab", left_im, right, preferred_element_type=jnp.float32)
    cross = jnp.concatenate([cross_re, cross_im], axis=0).astype(jnp.bfloat16)
    summed = jnp.einsum("kab,kt->abt", cross, table, preferred_element_type=jnp.float32)
    return summed * norm


def silent_block(rows_count, width):
    return jnp.zeros((rows_count, width, LAGS), jnp.float32)


def per_device(spectra, half_width, band):
    white = whiten(spectra, half_width)
    own = lax.all_gather(white, "seg", axis=1, tiled=True)
    width = own.shape[3]
    rows_count = width // lax.axis_size("seg")
    seg_index = lax.axis_index("seg")
    rows = lax.dynamic_slice_in_dim(own, seg_index * rows_count, rows_count, 3)
    near = shifted(own, "chan", -1)
    far = shifted(own, "chan", -2)
    table = lag_table(half_width.shape[0], LAGS)
    norm = 1.0 / math.sqrt(own.shape[1] * half_width.shape[0])
    chan_index = lax.axis_index("chan")
    blocks = lax.axis_size("chan")
    my_band = jnp.sum(jnp.where(jnp.arange(blocks, dtype=jnp.int32) == chan_index, band, 0))
    results = []
    for offset, partner in enumerate((own, near, far)):
        live = (offset <= my_band) & (chan_index + offset < blocks)
        value = lax.cond(
            live,
            partial(cross_lags, rows, partner, table, norm),
            partial(silent_block, rows_count, width),
        )
        results.append(value)
    return jnp.stack(results, axis=1)


def solution(mesh):
    in_specs = (P(None, "seg", None, "chan"), P(), P())
    out_specs = P(("chan", "seg"), None, None, None)
    return jax.shard_map(
        per_device, mesh=mesh, in_specs=in_specs, out_specs=out_specs, check_vma=False
    )
```

profile of v0, /device:TPU:115, one launch (start us, length us, event | category | flops | bytes accessed | tf_op | source)
XLA Modules:
  0.0 598.5 jit_solution(9929326595649568844)
XLA Ops:
  14.5 64.7 %all-gather.2.cloned.1.call-done = bf16[2,16,768,128]{3,2,1,0:T(8,128)(2,1)} async-done(((bf16[2,4,768,128]{3,2,1,0:T(8,128)(2,1)}), bf16[2,16,768,128]{3,2,1,0:T(8,128)(2,1)}) %all-gather.2.cloned.1.call-update) | async-done | bytes 6291472 | tf_op jit(solution)/shard_map/all_gather | solution.py:80
  100.5 86.7 %conditional.3 = (f32[32,1,128,256]{3,2,0,1:T(8,128)}) conditional(s32[]{:T(128)} %convert_element_type.34, () %tuple.29, (bf16[2,16,768,32]{3,2,1,0:T(8,128)(2,1)}, bf16[2,16,768,128]{3,2,1,0:T(8,128)(2,1)}, bf16[1536,256]{1,0:T(8,128)(2,1)}) %tuple.30), branch_computations={%region_1.2_spmd, %region_2.3_spmd} | conditional | flops 3655204864 | bytes 144179264 | solution.py:95
  107.4 11.9 %copy.13 = bf16[32,768,32]{0,2,1:T(8,128)(2,1)} copy(bf16[32,768,32]{1,2,0:T(8,128)(2,1)} %get-tuple-element.57) | data formatting | bytes 3145728 | tf_op jit(solution)/shard_map/cond/branch_1_fun/concatenate | solution.py:64
  129.5 9.8 %fusion.6 = bf16[768,32,128]{2,1,0:T(8,128)(2,1)} fusion(bf16[32,768,32]{0,2,1:T(8,128)(2,1)} %copy.13, bf16[32,768,128]{2,1,0:T(8,128)(2,1)S(1)} %pad_maximum_fusion), kind=kOutput, calls=%fused_computation.7 | convolution fusion | flops 201326592 | bytes 14155776 | tf_op jit(solution)/shard_map/cond/branch_1_fun/ska,skb->kab/dot_general | solution.py:67
  139.3 9.2 %copy.15 = bf16[768,32,128]{0,2,1:T(8,128)(2,1)} copy(bf16[768,32,128]{2,1,0:T(8,128)(2,1)} %fusion.6) | data formatting | bytes 12582912 | tf_op jit(solution)/shard_map/cond/branch_1_fun/ska,skb->kab/dot_general | solution.py:67
  148.5 10.0 %copy.16 = bf16[32,768,32]{0,2,1:T(8,128)(2,1)} copy(bf16[32,768,32]{1,2,0:T(8,128)(2,1)S(1)} %get-tuple-element.58) | data formatting | bytes 3145728 | tf_op jit(solution)/shard_map/cond/branch_1_fun/concatenate | solution.py:65
  158.5 11.4 %fusion.4 = bf16[768,32,128]{2,1,0:T(8,128)(2,1)} fusion(bf16[32,768,32]{0,2,1:T(8,128)(2,1)} %copy.16, bf16[32,768,128]{2,1,0:T(8,128)(2,1)} %copy-done), kind=kOutput, calls=%fused_computation.5 | convolution fusion | flops 201326592 | bytes 14155776 | tf_op jit(solution)/shard_map/cond/branch_1_fun/ska,skb->kab/dot_general | solution.py:68
  169.9 9.3 %copy.17 = bf16[768,32,128]{0,2,1:T(8,128)(2,1)} copy(bf16[768,32,128]{2,1,0:T(8,128)(2,1)} %fusion.4) | data formatting | bytes 12582912 | tf_op jit(solution)/shard_map/cond/branch_1_fun/ska,skb->kab/dot_general | solution.py:68
  187.2 31.5 %collective-permute-done = bf16[2,16,768,128]{3,2,1,0:T(8,128)(2,1)} collective-permute-done((bf16[2,16,768,128]{3,2,1,0:T(8,128)(2,1)}, bf16[2,16,768,128]{3,2,1,0:T(8,128)(2,1)}, u32[]{:S(2)}, u32[]{:S(2)}) %collective-permute-start) | collective-permute-done | bytes 6291488 | tf_op jit(solution)/shard_map/ppermute | solution.py:21
  218.8 86.8 %conditional.4 = (f32[32,1,128,256]{3,2,0,1:T(8,128)}) conditional(s32[]{:T(128)} %convert_element_type.39, () %tuple.31, (bf16[2,16,768,32]{3,2,1,0:T(8,128)(2,1)}, bf16[2,16,768,128]{3,2,1,0:T(8,128)(2,1)}, bf16[1536,256]{1,0:T(8,128)(2,1)}) %tuple.32), branch_computations={%region_3.4_spmd, %region_4.5_spmd} | conditional | flops 3655204864 | bytes 144179264 | solution.py:95
  225.6 11.9 %copy.18 = bf16[32,768,32]{0,2,1:T(8,128)(2,1)} copy(bf16[32,768,32]{1,2,0:T(8,128)(2,1)} %get-tuple-element.63) | data formatting | bytes 3145728 | tf_op jit(solution)/shard_map/cond/branch_1_fun/concatenate | solution.py:64
  247.7 9.8 %fusion.19 = bf16[768,32,128]{2,1,0:T(8,128)(2,1)} fusion(bf16[32,768,32]{0,2,1:T(8,128)(2,1)} %copy.18, bf16[32,768,128]{2,1,0:T(8,128)(2,1)S(1)} %pad_maximum_fusion.3), kind=kOutput, calls=%fused_computation.26 | convolution fusion | flops 201326592 | bytes 14155776 | tf_op jit(solution)/shard_map/cond/branch_1_fun/ska,skb->kab/dot_general | solution.py:67
  266.7 10.2 %copy.21 = bf16[32,768,32]{0,2,1:T(8,128)(2,1)} copy(bf16[32,768,32]{1,2,0:T(8,128)(2,1)S(1)} %get-tuple-element.64) | data formatting | bytes 3145728 | tf_op jit(solution)/shard_map/cond/branch_1_fun/concatenate | solution.py:65
  276.9 11.4 %fusion.17 = bf16[768,32,128]{2,1,0:T(8,128)(2,1)} fusion(bf16[32,768,32]{0,2,1:T(8,128)(2,1)} %copy.21, bf16[32,768,128]{2,1,0:T(8,128)(2,1)} %copy-done.1), kind=kOutput, calls=%fused_computation.24 | convolution fusion | flops 201326592 | bytes 14155776 | tf_op jit(solution)/shard_map/cond/branch_1_fun/ska,skb->kab/dot_general | solution.py:68
  288.3 9.3 %copy.22 = bf16[768,32,128]{0,2,1:T(8,128)(2,1)} copy(bf16[768,32,128]{2,1,0:T(8,128)(2,1)} %fusion.17) | data formatting | bytes 12582912 | tf_op jit(solution)/shard_map/cond/branch_1_fun/ska,skb->kab/dot_general | solution.py:68
  305.6 188.5 %collective-permute-done.1 = bf16[2,16,768,128]{3,2,1,0:T(8,128)(2,1)} collective-permute-done((bf16[2,16,768,128]{3,2,1,0:T(8,128)(2,1)}, bf16[2,16,768,128]{3,2,1,0:T(8,128)(2,1)}, u32[]{:S(2)}, u32[]{:S(2)}) %collective-permute-start.1) | collective-permute-done | bytes 6291488 | tf_op jit(solution)/shard_map/ppermute | solution.py:21
  494.1 86.3 %conditional.5 = (f32[32,1,128,256]{3,2,0,1:T(8,128)}) conditional(s32[]{:T(128)} %convert_element_type.40, () %tuple.33, (bf16[2,16,768,32]{3,2,1,0:T(8,128)(2,1)}, bf16[2,16,768,128]{3,2,1,0:T(8,128)(2,1)}, bf16[1536,256]{1,0:T(8,128)(2,1)}) %tuple.34), branch_computations={%region_5.6_spmd, %region_6.7_spmd} | conditional | flops 3655204864 | bytes 144179264 | solution.py:95
  500.8 11.9 %copy.23 = bf16[32,768,32]{0,2,1:T(8,128)(2,1)} copy(bf16[32,768,32]{1,2,0:T(8,128)(2,1)} %get-tuple-element.69) | data formatting | bytes 3145728 | tf_op jit(solution)/shard_map/cond/branch_1_fun/concatenate | solution.py:64
  522.8 9.7 %fusion.32 = bf16[768,32,128]{2,1,0:T(8,128)(2,1)} fusion(bf16[32,768,32]{0,2,1:T(8,128)(2,1)} %copy.23, bf16[32,768,128]{2,1,0:T(8,128)(2,1)S(1)} %pad_maximum_fusion.6), kind=kOutput, calls=%fused_computation.45 | convolution fusion | flops 201326592 | bytes 14155776 | tf_op jit(solution)/shard_map/cond/branch_1_fun/ska,skb->kab/dot_general | solution.py:67
  532.5 9.3 %copy.25 = bf16[768,32,128]{0,2,1:T(8,128)(2,1)} copy(bf16[768,32,128]{2,1,0:T(8,128)(2,1)} %fusion.32) | data formatting | bytes 12582912 | tf_op jit(solution)/shard_map/cond/branch_1_fun/ska,skb->kab/dot_general | solution.py:67
  541.7 9.9 %copy.26 = bf16[32,768,32]{0,2,1:T(8,128)(2,1)} copy(bf16[32,768,32]{1,2,0:T(8,128)(2,1)S(1)} %get-tuple-element.70) | data formatting | bytes 3145728 | tf_op jit(solution)/shard_map/cond/branch_1_fun/concatenate | solution.py:65
  551.7 11.3 %fusion.30 = bf16[768,32,128]{2,1,0:T(8,128)(2,1)} fusion(bf16[32,768,32]{0,2,1:T(8,128)(2,1)} %copy.26, bf16[32,768,128]{2,1,0:T(8,128)(2,1)} %copy-done.2), kind=kOutput, calls=%fused_computation.43 | convolution fusion | flops 201326592 | bytes 14155776 | tf_op jit(solution)/shard_map/cond/branch_1_fun/ska,skb->kab/dot_general | solution.py:68
  563.0 9.3 %copy.27 = bf16[768,32,128]{0,2,1:T(8,128)(2,1)} copy(bf16[768,32,128]{2,1,0:T(8,128)(2,1)} %fusion.30) | data formatting | bytes 12582912 | tf_op jit(solution)/shard_map/cond/branch_1_fun/ska,skb->kab/dot_general | solution.py:68
  580.4 11.0 %pad_maximum_fusion.9 = f32[32,3,128,256]{3,2,1,0:T(8,128)} fusion(f32[32,1,128,256]{3,2,1,0:T(8,128)} %bitcast.112, f32[32,1,128,256]{3,2,1,0:T(8,128)} %bitcast.111, f32[32,1,128,256]{3,2,1,0:T(8,128)} %bitcast.110), kind=kLoop, calls=%fused_computation.57 | loop fusion | flops 6291456 | bytes 25165824 | tf_op jit(solution)/shard_map/stack | solution.py:101
  (66 shorter events, 110.5 us)
Async XLA Ops:
  6.5 72.7 %all-gather.2.cloned.1.call-start = ((), (), s32[]{:S(2)}) async-start(), calls=%async_computation | async-start | bytes 7864320 | tf_op jit(solution)/shard_map/all_gather | solution.py:80
  7.3 5.5 copy-start.3
  12.8 73.2 %copy-start.7 = (s32[32]{0:T(128)S(1)}, s32[32]{0:T(128)}, u32[]{:S(2)}) copy-start(s32[32]{0:T(128)} %param.11) | copy-start | bytes 388
  79.2 139.6 %collective-permute-start = (bf16[2,16,768,128]{3,2,1,0:T(8,128)(2,1)}, bf16[2,16,768,128]{3,2,1,0:T(8,128)(2,1)}, u32[]{:S(2)}, u32[]{:S(2)}) collective-permute-start(bf16[2,16,768,128]{3,2,1,0:T(8,128)(2,1)} %all-gather.2.cloned.1.call-done), channel_id=1, source_target_pairs={{4,0},{8,4},{12,8},{16,12},{20,16},{24,20},{28,24},{32,28},{36,32}... | collective-permute-start | bytes 18874376 | tf_op jit(solution)/shard_map/ppermute | solution.py:21
  81.4 412.7 %collective-permute-start.1 = (bf16[2,16,768,128]{3,2,1,0:T(8,128)(2,1)}, bf16[2,16,768,128]{3,2,1,0:T(8,128)(2,1)}, u32[]{:S(2)}, u32[]{:S(2)}) collective-permute-start(bf16[2,16,768,128]{3,2,1,0:T(8,128)(2,1)} %all-gather.2.cloned.1.call-done), channel_id=1, source_target_pairs={{8,0},{12,4},{16,8},{20,12},{24,16},{28,20},{32,24},{36,28},{40,32... | collective-permute-start | bytes 18874376 | tf_op jit(solution)/shard_map/ppermute | solution.py:21
  126.8 2.7 copy-start
  169.9 9.3 %copy-start.4 = (bf16[1536,256]{1,0:T(8,128)(2,1)S(1)}, bf16[1536,256]{1,0:T(8,128)(2,1)}, u32[]{:S(2)}) copy-start(bf16[1536,256]{1,0:T(8,128)(2,1)} %get-tuple-element.37) | copy-start | bytes 2359300 | tf_op jit(solution)/shard_map/cond
  245.0 2.7 copy-start.1
  288.3 9.3 %copy-start.5 = (bf16[1536,256]{1,0:T(8,128)(2,1)S(1)}, bf16[1536,256]{1,0:T(8,128)(2,1)}, u32[]{:S(2)}) copy-start(bf16[1536,256]{1,0:T(8,128)(2,1)} %get-tuple-element.40) | copy-start | bytes 2359300 | tf_op jit(solution)/shard_map/cond
  520.2 2.6 copy-start.2
  563.0 9.3 %copy-start.6 = (bf16[1536,256]{1,0:T(8,128)(2,1)S(1)}, bf16[1536,256]{1,0:T(8,128)(2,1)}, u32[]{:S(2)}) copy-start(bf16[1536,256]{1,0:T(8,128)(2,1)} %get-tuple-element.43) | copy-start | bytes 2359300 | tf_op jit(solution)/shard_map/cond
Sparse Core Ops, SparseCore 0:
  14.7 64.5 all-gather.1
where the time goes:
time: 606 us; the launch traced here: 599 us
  waiting for transfers between devices  285 us (47%)
  local copies, waits for them, and re-layouts  167 us (28%)
  matrix products  90.3 us (15%)
  other arithmetic  32.6 us (5%)
  between operations  15.8 us (3%)
  starting transfers between devices  6.71 us (1%)
    ppermute x2, waiting for transfers between devices, shifted(): return lax.ppermute(array, axis, pairs)  220 us
    all_gather x1, waiting for transfers between devices, per_device(): own = lax.all_gather(white, 'seg', axis=1, tiled=True)  64.7 us
    concatenate x3, local copies, waits for them, and re-layouts, cross_lags(): left_re = jnp.concatenate([rows[0], rows[1]], axis=0)  35.8 us
    dot_general x3, matrix products, cross_lags(): jnp.einsum('ska,skb->kab', left_im, right, preferred_element_type=jnp.flo...  34.1 us
    concatenate x3, local copies, waits for them, and re-layouts, cross_lags(): left_im = jnp.concatenate([rows[1], -rows[0]], axis=0)  30.1 us
    dot_general x3, matrix products, cross_lags(): jnp.einsum('ska,skb->kab', left_re, right, preferred_element_type=jnp.flo...  29.3 us
    dot_general x3, local copies, waits for them, and re-layouts, cross_lags(): jnp.einsum('ska,skb->kab', left_im, right, preferred_element_type=jnp.flo...  27.9 us
    dot_general x3, local copies, waits for them, and re-layouts, cross_lags(): jnp.einsum('ska,skb->kab', left_re, right, preferred_element_type=jnp.flo...  27.7 us
  transfers between devices with their start and end apart: 3, of which 3 were waited for; matrix products, arithmetic and copies ran while one was open for 30% of the time, Pallas kernels for 0%

commit v1 on v0

v1 whole, which is shorter than its diff:
```python
from functools import partial
import math

import jax
import jax.numpy as jnp
import numpy as np
from jax import lax
from jax.experimental import pallas as pl
from jax.experimental.pallas import tpu as pltpu
from jax.sharding import PartitionSpec as P

FLO = 25
NT = 3000
LAGS = 256
BINS = 768
BLOCKS = 32
CH = 128
ROWS = 32
REACH = 16
FLOOR = 0.2

PIECES = 12
GROUPS = 8
SPAN = 128
STEPS = BINS // SPAN

MESH = pl.DeviceIdType.MESH
f32 = jnp.float32
bf16 = jnp.bfloat16

(OWN_SIB, OWN_X, NEAR, LEG1, OWN2_SIB, NEAR2, NEAR_SIB, NEAR2_SIB, LEG2, FAR_SIB, FAR_X, FAR2_SIB) = range(12)
FLOWS = 12


def lag_table():
    index = np.arange(BINS, dtype=np.int64)
    shifts = np.arange(LAGS, dtype=np.int64) - LAGS // 2 + 1
    phase = ((FLO + index)[:, None] * shifts[None, :]) % NT
    angle = np.float32(2.0 * math.pi / NT) * phase.astype(np.float32)
    angle = angle.astype(np.float64)
    table = np.stack([np.cos(angle), -np.sin(angle)])
    table = table.reshape(2, STEPS, SPAN, LAGS).transpose(1, 3, 0, 2).reshape(STEPS, LAGS, 2 * SPAN)
    return table.astype(np.float32).astype(jnp.bfloat16)


def dot(a, b):
    return lax.dot_general(a, b, (((1,), (0,)), ((), ())), preferred_element_type=f32)


def dot_nt(a, b):
    return lax.dot_general(a, b, (((1,), (1,)), ((), ())), preferred_element_type=f32)


def kernel(
    norm, spec, half, band, table, out,
    white, relay, amp_hi, amp_lo, turned, pick, diag, cross, acc0, acc, ssem, rsem, osem0, osem,
):
    c = lax.axis_index("chan")
    s = lax.axis_index("seg")
    xl = s // 2
    xq = (s + 2) % 4

    def block_at(d):
        t = lax.rem(c + d + 2 * BLOCKS, BLOCKS)
        return t, jnp.where(t // 16 != c // 16, xq, s)

    sib = (c, xl * 2 + 1 - s % 2)
    across = (c, xq)
    near_to = block_at(-1)
    near_from = block_at(1)
    even = c % 2 == 0
    leg_to = block_at(jnp.where(even, 1, -3))
    leg_from = block_at(jnp.where(even, 3, -1))
    nq = near_from[1]
    nq2 = (nq + 2) % 4
    fq = block_at(2)[1]
    fq2 = (fq + 2) % 4
    rq = leg_from[1]

    barrier = pltpu.get_barrier_semaphore()
    for d in (sib, across, near_to, near_from, leg_to, leg_from):
        pl.semaphore_signal(barrier, inc=1, device_id=d, device_id_type=MESH)
    pl.semaphore_wait(barrier, 6)

    def copy(flow, j):
        here, there, to = {
            OWN_SIB: ((0, s), (0, s), sib),
            OWN_X: ((0, s), (0, s), across),
            NEAR: ((0, s), (1, s), near_to),
            LEG1: ((0, s), None, leg_to),
            OWN2_SIB: ((0, xq), (0, xq), sib),
            NEAR2: ((0, xq), (1, xq), near_to),
            NEAR_SIB: ((1, nq), (1, nq), sib),
            NEAR2_SIB: ((1, nq2), (1, nq2), sib),
            LEG2: (None, (2, rq), leg_to),
            FAR_SIB: ((2, fq), (2, fq), sib),
            FAR_X: ((2, fq), (2, fq), across),
            FAR2_SIB: ((2, fq2), (2, fq2), sib),
        }[flow]
        place = lambda at: relay.at[j] if at is None else white.at[at[0], j, :, at[1]]
        return pltpu.make_async_remote_copy(
            src_ref=place(here), dst_ref=place(there), send_sem=ssem.at[flow, j], recv_sem=rsem.at[flow, j],
            device_id=to, device_id_type=MESH,
        )

    amp_hi[pl.ds(0, REACH), :] = jnp.zeros((REACH, 4 * CH), bf16)
    amp_lo[pl.ds(0, REACH), :] = jnp.zeros((REACH, 4 * CH), bf16)
    amp_hi[pl.ds(REACH + BINS, SPAN - REACH), :] = jnp.zeros((SPAN - REACH, 4 * CH), bf16)
    amp_lo[pl.ds(REACH + BINS, SPAN - REACH), :] = jnp.zeros((SPAN - REACH, 4 * CH), bf16)

    def amplitude(m, carry):
        rows = pl.ds(pl.multiple_of(m * SPAN, SPAN), SPAN)
        to = pl.ds(pl.multiple_of(m * SPAN + REACH, REACH), SPAN)
        for seg in range(4):
            re = spec[0, seg, rows, :].astype(f32)
            im = spec[1, seg, rows, :].astype(f32)
            a = jnp.sqrt(re * re + im * im)
            hi = a.astype(bf16)
            amp_hi[to, seg * CH : (seg + 1) * CH] = hi
            amp_lo[to, seg * CH : (seg + 1) * CH] = (a - hi.astype(f32)).astype(bf16)
        return carry

    lax.fori_loop(0, STEPS, amplitude, 0)

    def whiten(m, carry):
        rows = pl.ds(pl.multiple_of(m * SPAN, SPAN), SPAN)
        window = pl.ds(pl.multiple_of(m * SPAN, SPAN), 2 * SPAN)
        width = jnp.broadcast_to(half[pl.ds(m, 1), :].astype(f32), (SPAN, SPAN)).T
        width2 = jnp.concatenate([width, width], axis=1)
        row = lax.broadcasted_iota(jnp.int32, (SPAN, 2 * SPAN), 0)
        col = lax.broadcasted_iota(jnp.int32, (SPAN, 2 * SPAN), 1)
        inside = jnp.abs(col - REACH - row).astype(f32) <= width2
        inside = jnp.where(inside, 1.0, 0.0).astype(bf16)
        bin_at = (lax.broadcasted_iota(jnp.int32, (SPAN, SPAN), 0) + m * SPAN).astype(f32)
        count = jnp.minimum(bin_at + width, BINS - 1.0) - jnp.maximum(bin_at - width, 0.0) + 1.0
        total = dot(inside, amp_hi[window, :]) + dot(inside, amp_lo[window, :])
        for seg in range(4):
            denom = jnp.maximum(total[:, seg * CH : (seg + 1) * CH] / count, FLOOR)
            for part in range(2):
                turned[pl.ds((part * 4 + seg) * SPAN, SPAN), :] = spec[part, seg, rows, :].astype(f32) / denom
        for b in range(SPAN // 16):
            block = [turned[pl.ds(b * 16 + t, 8, stride=SPAN), :] for t in range(16)]
            block = jnp.concatenate(block, axis=0).astype(bf16)
            j = m * 2 + b // 4
            white[0, j, (b % 4) * 2, s] = block[:64]
            white[0, j, (b % 4) * 2 + 1, s] = block[64:]
        for j in (m * 2, m * 2 + 1):
            for flow in (OWN_X, NEAR, LEG1, OWN_SIB):
                copy(flow, j).start()
        return carry

    lax.fori_loop(0, STEPS, whiten, 0)

    row = lax.broadcasted_iota(jnp.int32, (8 * ROWS, CH), 0)
    col = lax.broadcasted_iota(jnp.int32, (8 * ROWS, CH), 1)
    pick[...] = jnp.where(col == s * ROWS + row // 8, 1.0, 0.0).astype(bf16)
    row = lax.broadcasted_iota(jnp.int32, (8 * ROWS, 256), 0)
    col = lax.broadcasted_iota(jnp.int32, (8 * ROWS, 256), 1)
    diag[...] = jnp.where(row % 8 == (col // 8) % 8, 1.0, 0.0)

    def left(j, g):
        x = white[0, j, g].reshape(256, CH)
        y = x.astype(f32).reshape(32, 8, CH)
        y = jnp.concatenate([y[:, 4:], -y[:, :4]], axis=1).reshape(256, CH).astype(bf16)
        keep = diag[...]
        re = (dot_nt(pick[...], x) * keep).astype(bf16)
        im = (dot_nt(pick[...], y) * keep).astype(bf16)
        return jnp.concatenate([re, im], axis=0)

    def crosses(j, g, slots):
        both = []
        for u in (g, g + 1):
            right = [white[d, j, u].reshape(256, CH) for d in slots]
            right = right[0] if len(right) == 1 else jnp.concatenate(right, axis=1)
            both.append(dot(left(j, u), right).reshape(2 * ROWS, 8, right.shape[1]))
        return jnp.concatenate(both, axis=1).astype(bf16)

    def project(j, count, into, first, last, finish):
        def one(p, carry):
            got = dot(table[j // 2], cross[p])
            if not first:
                got = got + into[p]
            if last:
                into[p] = (got * norm).T
                finish(p)
            else:
                into[p] = got
            return carry

        lax.fori_loop(0, count, one, 0)

    def project_at(j, count, into, mask, finish):
        @pl.when(j == 1)
        def _():
            project(j, count, into, True, False, finish)

        @pl.when((j % 2 == 1) & (j > 1) & (j < PIECES - 1))
        def _():
            project(j, count, into, False, False, finish)

        @pl.when(j == PIECES - 1)
        def _():
            project(j, count, into, False, True, finish)

    def out0(p, h):
        return pltpu.make_async_copy(acc0.at[p, pl.ds(h * CH, CH)], out.at[2 * p + h, 0], osem0.at[p, h])

    def finish0(p):
        for h in range(2):
            out0(p, h).start()

    def compute0(j):
        copy(OWN_SIB, j).wait_recv()
        copy(OWN2_SIB, j).wait_recv()

        def pair(i, carry):
            got = crosses(j, 2 * i, (0,)).reshape(2, ROWS // 2, 2, 16, CH)
            at = (j % 2) * 64 + i * 16
            for part in range(2):
                for h in range(2):
                    bins = pl.ds(pl.multiple_of(part * SPAN + at, 16), 16)
                    cross[pl.ds(0, ROWS // 2), bins, h * CH : (h + 1) * CH] = got[part, :, h]
            return carry

        lax.fori_loop(0, GROUPS // 2, pair, 0)
        project_at(j, ROWS // 2, acc0, None, finish0)

    reach = jnp.minimum(band[c], BLOCKS - 1 - c)

    def out12(p, h):
        return pltpu.make_async_copy(acc.at[p, pl.ds(h * CH, CH)], out.at[p, 1 + h], osem.at[p, h])

    def finish12(p):
        for h in range(2):
            rows = pl.ds(h * CH, CH)
            live = jnp.full((CH, LAGS), reach, jnp.int32) >= h + 1
            acc[p, rows] = jnp.where(live, acc[p, rows], 0.0)
            out12(p, h).start()

    def compute12(j):
        for flow in (NEAR_SIB, NEAR2_SIB, FAR_SIB, FAR2_SIB):
            copy(flow, j).wait_recv()

        def pair(i, carry):
            got = crosses(j, 2 * i, (1, 2)).reshape(2, ROWS, 16, 2 * CH)
            at = (j % 2) * 64 + i * 16
            for part in range(2):
                bins = pl.ds(pl.multiple_of(part * SPAN + at, 16), 16)
                cross[:, bins, :] = got[part]
            return carry

        lax.fori_loop(0, GROUPS // 2, pair, 0)
        project_at(j, ROWS, acc, None, finish12)

    def first_half(j, carry):
        copy(OWN_X, j).wait_recv()
        copy(NEAR2, j).start()
        copy(OWN2_SIB, j).start()
        copy(LEG1, j).wait_recv()
        copy(LEG2, j).start()
        copy(NEAR, j).wait_recv()
        copy(NEAR_SIB, j).start()

        @pl.when(j > 0)
        def _():
            compute0(j - 1)

        return carry

    lax.fori_loop(0, PIECES, first_half, 0)
    compute0(PIECES - 1)

    def far_across(j):
        copy(FAR_X, j).wait_recv()
        copy(FAR2_SIB, j).start()

    def second_half(j, carry):
        copy(LEG2, j).wait_recv()
        copy(FAR_X, j).start()
        copy(FAR_SIB, j).start()
        copy(NEAR2, j).wait_recv()
        copy(NEAR2_SIB, j).start()

        @pl.when(j > 0)
        def _():
            far_across(j - 1)

        @pl.when(j > 1)
        def _():
            compute12(j - 2)

        return carry

    lax.fori_loop(0, PIECES, second_half, 0)
    compute12(PIECES - 2)
    far_across(PIECES - 1)
    compute12(PIECES - 1)

    def sent(j, carry):
        for flow in range(FLOWS):
            copy(flow, j).wait_send()
        return carry

    lax.fori_loop(0, PIECES, sent, 0)

    def written(p, carry):
        for h in range(2):
            out12(p, h).wait()
        return carry

    lax.fori_loop(0, ROWS, written, 0)

    def written0(p, carry):
        for h in range(2):
            out0(p, h).wait()
        return carry

    lax.fori_loop(0, ROWS // 2, written0, 0)


def per_device(table, spectra, half_width, band):
    norm = 1.0 / math.sqrt(4 * spectra.shape[1] * BINS)
    vmem = pl.BlockSpec(memory_space=pltpu.VMEM)
    return pl.pallas_call(
        partial(kernel, norm),
        out_shape=jax.ShapeDtypeStruct((ROWS, 3, CH, LAGS), f32),
        in_specs=[vmem, vmem, pl.BlockSpec(memory_space=pltpu.SMEM), vmem],
        out_specs=pl.BlockSpec(memory_space=pl.ANY),
        scratch_shapes=[
            pltpu.VMEM((3, PIECES, GROUPS, 4, 64, CH), bf16),
            pltpu.VMEM((PIECES, GROUPS, 64, CH), bf16),
            pltpu.VMEM((BINS + SPAN, 4 * CH), bf16),
            pltpu.VMEM((BINS + SPAN, 4 * CH), bf16),
            pltpu.VMEM((8 * SPAN, CH), f32),
            pltpu.VMEM((8 * ROWS, CH), bf16),
            pltpu.VMEM((8 * ROWS, 256), f32),
            pltpu.VMEM((ROWS, 2 * SPAN, 2 * CH), bf16),
            pltpu.VMEM((ROWS // 2, LAGS, 2 * CH), f32),
            pltpu.VMEM((ROWS, LAGS, 2 * CH), f32),
            pltpu.SemaphoreType.DMA((FLOWS, PIECES)),
            pltpu.SemaphoreType.DMA((FLOWS, PIECES)),
            pltpu.SemaphoreType.DMA((ROWS // 2, 2)),
            pltpu.SemaphoreType.DMA((ROWS, 2)),
        ],
        compiler_params=pltpu.CompilerParams(collective_id=0, has_side_effects=True, vmem_limit_bytes=60 * 2**20),
        cost_estimate=pl.CostEstimate(flops=2 * 5_500_000_000, bytes_accessed=16_000_000, transcendentals=0),
    )(spectra, half_width.reshape(STEPS, SPAN), band, table)


def solution(mesh):
    table = lag_table()

    def body(spectra, half_width, band):
        return per_device(jnp.asarray(table), spectra, half_width, band)

    in_specs = (P(None, "seg", None, "chan"), P(), P())
    out_specs = P(("chan", "seg"), None, None, None)
    return jax.shard_map(body, mesh=mesh, in_specs=in_specs, out_specs=out_specs, check_vma=False)
```

time: 606 us -> 168 us (0.28)
  the two profiles are of different devices: /device:TPU:115 before, /device:TPU:1 now
where the time goes in v1:
time: 168 us
  Pallas kernels  157 us (93%)
  local copies, waits for them, and re-layouts  10.9 us (6%)
    pallas_call x1, Pallas kernels, per_device(): pl.pallas_call(partial(kernel, norm), out_shape=jax.ShapeDtypeStruct((ROW...  157 us
    unnamed x1, local copies, waits for them, and re-layouts  10.9 us

profile of v1, /device:TPU:1, one launch (start us, length us, event | category | flops | bytes accessed | tf_op | source)
XLA Modules:
  0.0 168.2 jit_solution(15108917495139122873)
XLA Ops:
  0.0 157.2 %shard_map.46 = f32[32,3,128,256]{3,2,1,0:T(8,128)} custom-call(bf16[2,4,768,128]{3,2,1,0:T(8,128)(2,1)} %spec.1, s32[6,128]{1,0:T(8,128)} %bitcast.1, s32[32]{0:T(128)} %band.1, bf16[6,256,256]{2,1,0:T(8,128)(2,1)} %constant.2.clone.table), custom_call_target="tpu_custom_call" | custom-call | flops 11000000512 | bytes 16000000 | tf_op jit(solution)/shard_map/pallas_call | solution.py:324
  157.2 10.9 %copy.6 = f32[32,3,128,256]{3,2,1,0:T(8,128)} copy(f32[32,3,128,256]{3,2,1,0:T(8,128)} %shard_map.46) | data formatting | bytes 25165824

commit v2 on v1

--- a/solution.py
+++ b/solution.py
@@ -23,6 +23,7 @@
 GROUPS = 8
 SPAN = 128
 STEPS = BINS // SPAN
+VMEM_GATHER = 44 * 2**20
 
 MESH = pl.DeviceIdType.MESH
 f32 = jnp.float32
@@ -51,9 +52,9 @@
     return lax.dot_general(a, b, (((1,), (1,)), ((), ())), preferred_element_type=f32)
 
 
-def kernel(
-    norm, spec, half, band, table, out,
-    white, relay, amp_hi, amp_lo, turned, pick, diag, cross, acc0, acc, ssem, rsem, osem0, osem,
+def gather(
+    spec, half, table, acc0, acc,
+    white, relay, amp_hi, amp_lo, turned, pick, diag, rows32, cross, ssem, rsem,
 ):
     c = lax.axis_index("chan")
     s = lax.axis_index("seg")
@@ -120,9 +121,13 @@
             amp_lo[to, seg * CH : (seg + 1) * CH] = (a - hi.astype(f32)).astype(bf16)
         return carry
 
-    lax.fori_loop(0, STEPS, amplitude, 0)
+    amplitude(0, 0)
 
     def whiten(m, carry):
+        @pl.when(m < STEPS - 1)
+        def _():
+            amplitude(m + 1, 0)
+
         rows = pl.ds(pl.multiple_of(m * SPAN, SPAN), SPAN)
         window = pl.ds(pl.multiple_of(m * SPAN, SPAN), 2 * SPAN)
         width = jnp.broadcast_to(half[pl.ds(m, 1), :].astype(f32), (SPAN, SPAN)).T
@@ -151,21 +156,24 @@
 
     lax.fori_loop(0, STEPS, whiten, 0)
 
-    row = lax.broadcasted_iota(jnp.int32, (8 * ROWS, CH), 0)
-    col = lax.broadcasted_iota(jnp.int32, (8 * ROWS, CH), 1)
-    pick[...] = jnp.where(col == s * ROWS + row // 8, 1.0, 0.0).astype(bf16)
-    row = lax.broadcasted_iota(jnp.int32, (8 * ROWS, 256), 0)
-    col = lax.broadcasted_iota(jnp.int32, (8 * ROWS, 256), 1)
-    diag[...] = jnp.where(row % 8 == (col // 8) % 8, 1.0, 0.0)
+    row = lax.broadcasted_iota(jnp.int32, (ROWS, CH), 0)
+    col = lax.broadcasted_iota(jnp.int32, (ROWS, CH), 1)
+    pick[...] = jnp.where(col == s * ROWS + row, 1.0, 0.0).astype(bf16)
+    row = lax.broadcasted_iota(jnp.int32, (8, 256), 0)
+    col = lax.broadcasted_iota(jnp.int32, (8, 256), 1)
+    diag[...] = jnp.where(row == (col // 8) % 8, 1.0, 0.0)
+
+    def turn_rows(j, g):
+        re = dot_nt(pick[...], white[0, j, g].reshape(256, CH))
+        col = lax.broadcasted_iota(jnp.int32, (ROWS, 256), 1)
+        rows32[j * GROUPS + g, :ROWS] = re
+        rows32[j * GROUPS + g, ROWS:] = jnp.where(col % 8 < 4, pltpu.roll(re, 252, 1), -pltpu.roll(re, 4, 1))
 
     def left(j, g):
-        x = white[0, j, g].reshape(256, CH)
-        y = x.astype(f32).reshape(32, 8, CH)
-        y = jnp.concatenate([y[:, 4:], -y[:, :4]], axis=1).reshape(256, CH).astype(bf16)
+        at = j * GROUPS + g
         keep = diag[...]
-        re = (dot_nt(pick[...], x) * keep).astype(bf16)
-        im = (dot_nt(pick[...], y) * keep).astype(bf16)
-        return jnp.concatenate([re, im], axis=0)
+        parts = [jnp.broadcast_to(rows32[at, pl.ds(r, 1), :], (8, 256)) * keep for r in range(2 * ROWS)]
+        return jnp.concatenate(parts, axis=0).astype(bf16)
 
     def crosses(j, g, slots):
         both = []
@@ -175,82 +183,48 @@
             both.append(dot(left(j, u), right).reshape(2 * ROWS, 8, right.shape[1]))
         return jnp.concatenate(both, axis=1).astype(bf16)
 
-    def project(j, count, into, first, last, finish):
-        def one(p, carry):
-            got = dot(table[j // 2], cross[p])
-            if not first:
-                got = got + into[p]
-            if last:
-                into[p] = (got * norm).T
-                finish(p)
-            else:
-                into[p] = got
+    def project(j, count, into, first):
+        def some(q, carry):
+            for u in range(8):
+                p = q * 8 + u
+                got = dot(table[j // 2], cross[p])
+                into[p] = got if first else into[p] + got
             return carry
 
-        lax.fori_loop(0, count, one, 0)
-
-    def project_at(j, count, into, mask, finish):
+        lax.fori_loop(0, count // 8, some, 0)
+
+    def project_at(j, count, into):
         @pl.when(j == 1)
         def _():
-            project(j, count, into, True, False, finish)
-
-        @pl.when((j % 2 == 1) & (j > 1) & (j < PIECES - 1))
-        def _():
-            project(j, count, into, False, False, finish)
-
-        @pl.when(j == PIECES - 1)
-        def _():
-            project(j, count, into, False, True, finish)
-
-    def out0(p, h):
-        return pltpu.make_async_copy(acc0.at[p, pl.ds(h * CH, CH)], out.at[2 * p + h, 0], osem0.at[p, h])
-
-    def finish0(p):
-        for h in range(2):
-            out0(p, h).start()
+            project(j, count, into, True)
+
+        @pl.when((j % 2 == 1) & (j > 1))
+        def _():
+            project(j, count, into, False)
+
+    def bins_at(j, i, part):
+        return pl.ds(pl.multiple_of(part * SPAN + (j % 2) * 64 + i * 16, 16), 16)
 
     def compute0(j):
         copy(OWN_SIB, j).wait_recv()
         copy(OWN2_SIB, j).wait_recv()
-
-        def pair(i, carry):
+        for g in range(GROUPS):
+            turn_rows(j, g)
+        for i in range(GROUPS // 2):
             got = crosses(j, 2 * i, (0,)).reshape(2, ROWS // 2, 2, 16, CH)
-            at = (j % 2) * 64 + i * 16
             for part in range(2):
                 for h in range(2):
-                    bins = pl.ds(pl.multiple_of(part * SPAN + at, 16), 16)
-                    cross[pl.ds(0, ROWS // 2), bins, h * CH : (h + 1) * CH] = got[part, :, h]
-            return carry
-
-        lax.fori_loop(0, GROUPS // 2, pair, 0)
-        project_at(j, ROWS // 2, acc0, None, finish0)
-
-    reach = jnp.minimum(band[c], BLOCKS - 1 - c)
-
-    def out12(p, h):
-        return pltpu.make_async_copy(acc.at[p, pl.ds(h * CH, CH)], out.at[p, 1 + h], osem.at[p, h])
-
-    def finish12(p):
-        for h in range(2):
-            rows = pl.ds(h * CH, CH)
-            live = jnp.full((CH, LAGS), reach, jnp.int32) >= h + 1
-            acc[p, rows] = jnp.where(live, acc[p, rows], 0.0)
-            out12(p, h).start()
+                    cross[pl.ds(0, ROWS // 2), bins_at(j, i, part), h * CH : (h + 1) * CH] = got[part, :, h]
+        project_at(j, ROWS // 2, acc0)
 
     def compute12(j):
         for flow in (NEAR_SIB, NEAR2_SIB, FAR_SIB, FAR2_SIB):
             copy(flow, j).wait_recv()
-
-        def pair(i, carry):
+        for i in range(GROUPS // 2):
             got = crosses(j, 2 * i, (1, 2)).reshape(2, ROWS, 16, 2 * CH)
-            at = (j % 2) * 64 + i * 16
             for part in range(2):
-                bins = pl.ds(pl.multiple_of(part * SPAN + at, 16), 16)
-                cross[:, bins, :] = got[part]
-            return carry
-
-        lax.fori_loop(0, GROUPS // 2, pair, 0)
-        project_at(j, ROWS, acc, None, finish12)
+                cross[:, bins_at(j, i, part), :] = got[part]
+        project_at(j, ROWS, acc)
 
     def first_half(j, carry):
         copy(OWN_X, j).wait_recv()
@@ -303,48 +277,56 @@
 
     lax.fori_loop(0, PIECES, sent, 0)
 
-    def written(p, carry):
-        for h in range(2):
-            out12(p, h).wait()
-        return carry
-
-    lax.fori_loop(0, ROWS, written, 0)
-
-    def written0(p, carry):
-        for h in range(2):
-            out0(p, h).wait()
-        return carry
-
-    lax.fori_loop(0, ROWS // 2, written0, 0)
+
+def finish(norm, band, acc0, acc, out):
+    c = lax.axis_index("chan")
+    reach = jnp.minimum(band[c], BLOCKS - 1 - c)
+    p = pl.program_id(0)
+    for h in range(2):
+        out[h, 0] = (acc0[p, :, h * CH : (h + 1) * CH] * norm).T
+        for d in (1, 2):
+            live = jnp.full((CH, LAGS), reach, jnp.int32) >= d
+            out[h, d] = jnp.where(live, (acc[2 * p + h, :, (d - 1) * CH : d * CH] * norm).T, 0.0)
 
 
 def per_device(table, spectra, half_width, band):
     norm = 1.0 / math.sqrt(4 * spectra.shape[1] * BINS)
     vmem = pl.BlockSpec(memory_space=pltpu.VMEM)
-    return pl.pallas_call(
-        partial(kernel, norm),
-        out_shape=jax.ShapeDtypeStruct((ROWS, 3, CH, LAGS), f32),
-        in_specs=[vmem, vmem, pl.BlockSpec(memory_space=pltpu.SMEM), vmem],
-        out_specs=pl.BlockSpec(memory_space=pl.ANY),
+    smem = pl.BlockSpec(memory_space=pltpu.SMEM)
+    acc0, acc = pl.pallas_call(
+        gather,
+        out_shape=[pltpu.VMEM((ROWS // 2, LAGS, 2 * CH), f32), pltpu.VMEM((ROWS, LAGS, 2 * CH), f32)],
+        in_specs=[vmem, vmem, vmem],
+        out_specs=[vmem, vmem],
         scratch_shapes=[
             pltpu.VMEM((3, PIECES, GROUPS, 4, 64, CH), bf16),
             pltpu.VMEM((PIECES, GROUPS, 64, CH), bf16),
             pltpu.VMEM((BINS + SPAN, 4 * CH), bf16),
             pltpu.VMEM((BINS + SPAN, 4 * CH), bf16),
             pltpu.VMEM((8 * SPAN, CH), f32),
-            pltpu.VMEM((8 * ROWS, CH), bf16),
-            pltpu.VMEM((8 * ROWS, 256), f32),
+            pltpu.VMEM((ROWS, CH), bf16),
+            pltpu.VMEM((8, 256), f32),
+            pltpu.VMEM((PIECES * GROUPS, 2 * ROWS, 256), f32),
             pltpu.VMEM((ROWS, 2 * SPAN, 2 * CH), bf16),
-            pltpu.VMEM((ROWS // 2, LAGS, 2 * CH), f32),
-            pltpu.VMEM((ROWS, LAGS, 2 * CH), f32),
             pltpu.SemaphoreType.DMA((FLOWS, PIECES)),
             pltpu.SemaphoreType.DMA((FLOWS, PIECES)),
-            pltpu.SemaphoreType.DMA((ROWS // 2, 2)),
-            pltpu.SemaphoreType.DMA((ROWS, 2)),
         ],
-        compiler_params=pltpu.CompilerParams(collective_id=0, has_side_effects=True, vmem_limit_bytes=60 * 2**20),
+        compiler_params=pltpu.CompilerParams(collective_id=0, has_side_effects=True, vmem_limit_bytes=VMEM_GATHER),
         cost_estimate=pl.CostEstimate(flops=2 * 5_500_000_000, bytes_accessed=16_000_000, transcendentals=0),
-    )(spectra, half_width.reshape(STEPS, SPAN), band, table)
+        name="gather",
+    )(spectra, half_width.reshape(STEPS, SPAN), table)
+    acc0 = pltpu.with_memory_space_constraint(acc0, pltpu.VMEM)
+    acc = pltpu.with_memory_space_constraint(acc, pltpu.VMEM)
+    return pl.pallas_call(
+        partial(finish, norm),
+        grid=(ROWS // 2,),
+        out_shape=jax.ShapeDtypeStruct((ROWS, 3, CH, LAGS), f32),
+        in_specs=[smem, vmem, vmem],
+        out_specs=pl.BlockSpec((2, 3, CH, LAGS), lambda p: (p, 0, 0, 0)),
+        compiler_params=pltpu.CompilerParams(vmem_limit_bytes=8 * 2**20),
+        cost_estimate=pl.CostEstimate(flops=0, bytes_accessed=12_600_000, transcendentals=0),
+        name="finish",
+    )(band, acc0, acc)
 
 
 def solution(mesh):

time: 168 us -> 109 us (0.65)
  Pallas kernels: 157 us -> 109 us
  local copies, waits for them, and re-layouts: 10.9 us -> 0.01 us
    pallas_call x1 -> x2, Pallas kernels: 157 us -> 109 us  [the longest x1 99.1 us: per_device(): pl.pallas_call(gather, out_shape=[pltpu.VMEM((ROWS // 2, LAGS, 2 * CH), f...]
    unnamed x1 -> x2, local copies, waits for them, and re-layouts: 10.9 us -> 0.01 us
where the time goes in v2:
time: 109 us
  Pallas kernels  109 us (100%)
    pallas_call x1, Pallas kernels, per_device(): pl.pallas_call(gather, out_shape=[pltpu.VMEM((ROWS // 2, LAGS, 2 * CH), f...  99.1 us
    pallas_call x1, Pallas kernels, per_device(): pl.pallas_call(partial(finish, norm), grid=(ROWS // 2,), out_shape=jax.Sh...  10.1 us

profile of v2, /device:TPU:1, one launch (start us, length us, event | category | flops | bytes accessed | tf_op | source)
XLA Modules:
  0.0 109.3 jit_solution(6807147349776724733)
XLA Ops:
  0.0 0.0 copy-start
  0.0 99.1 %gather.1 = (f32[16,256,256]{2,1,0:T(8,128)S(1)}, f32[32,256,256]{2,1,0:T(8,128)S(1)}) custom-call(bf16[2,4,768,128]{3,2,1,0:T(8,128)(2,1)} %spec.1, s32[6,128]{1,0:T(8,128)} %bitcast.1, bf16[6,256,256]{2,1,0:T(8,128)(2,1)} %constant.2.clone.table), custom_call_target="tpu_custom_call" | custom-call | flops 11000000512 | bytes 16000000 | tf_op jit(solution)/shard_map/gather/pallas_call | solution.py:296
  99.2 0.0 copy-done
  99.2 10.1 %finish.1 = f32[32,3,128,256]{3,2,1,0:T(8,128)} custom-call(s32[32]{0:T(128)S(1)} %copy-done, f32[16,256,256]{2,1,0:T(8,128)S(1)} %get-tuple-element.7.acc0, f32[32,256,256]{2,1,0:T(8,128)S(1)} %get-tuple-element.8.acc), custom_call_target="tpu_custom_call" | custom-call | bytes 12600000 | tf_op jit(solution)/shard_map/finish/pallas_call | solution.py:320
Async XLA Ops:
  0.0 99.2 %copy-start = (s32[32]{0:T(128)S(1)}, s32[32]{0:T(128)}, u32[]{:S(2)}) copy-start(s32[32]{0:T(128)} %band.1) | copy-start | bytes 388

commit v3 on v2

--- a/solution.py
+++ b/solution.py
@@ -20,10 +20,14 @@
 FLOOR = 0.2
 
 PIECES = 12
-GROUPS = 8
+WINDOW = 3
+LAG_FAR, LAG_ACROSS, LAG_LAST = 2, 4, 5
+GROUPS = BINS // 8 // PIECES
 SPAN = 128
 STEPS = BINS // SPAN
-VMEM_GATHER = 44 * 2**20
+SHARE = PIECES // STEPS
+VMEM_GATHER = 40 * 2**20
+VMEM_FINISH = 20 * 2**20
 
 MESH = pl.DeviceIdType.MESH
 f32 = jnp.float32
@@ -53,8 +57,8 @@
 
 
 def gather(
-    spec, half, table, acc0, acc,
-    white, relay, amp_hi, amp_lo, turned, pick, diag, rows32, cross, ssem, rsem,
+    spec, half, table, acc0, acc, cross,
+    white, relay, amp_hi, amp_lo, turned, pick, diag, rows32, cross0, ssem, rsem,
 ):
     c = lax.axis_index("chan")
     s = lax.axis_index("seg")
@@ -78,10 +82,21 @@
     fq2 = (fq + 2) % 4
     rq = leg_from[1]
 
+    sends_near, gets_near = c > 0, c < BLOCKS - 1
+    sends_far, gets_far = c > 1, c < BLOCKS - 2
+    relays = leg_from[0] > 1
+
     barrier = pltpu.get_barrier_semaphore()
-    for d in (sib, across, near_to, near_from, leg_to, leg_from):
-        pl.semaphore_signal(barrier, inc=1, device_id=d, device_id_type=MESH)
-    pl.semaphore_wait(barrier, 6)
+    greets = ((sib, None), (across, None), (near_to, sends_near), (near_from, gets_near), (leg_to, c != 1), (leg_from, c != BLOCKS - 2))
+    greeted = 0
+    for d, present in greets:
+        greet = partial(pl.semaphore_signal, barrier, inc=1, device_id=d, device_id_type=MESH)
+        if present is None:
+            greet()
+            greeted = greeted + 1
+        else:
+            pl.when(present)(greet)
+            greeted = greeted + present.astype(jnp.int32)
 
     def copy(flow, j):
         here, there, to = {
@@ -98,7 +113,7 @@
             FAR_X: ((2, fq), (2, fq), across),
             FAR2_SIB: ((2, fq2), (2, fq2), sib),
         }[flow]
-        place = lambda at: relay.at[j] if at is None else white.at[at[0], j, :, at[1]]
+        place = lambda at: relay.at[j] if at is None else white.at[at[0], j, at[1]]
         return pltpu.make_async_remote_copy(
             src_ref=place(here), dst_ref=place(there), send_sem=ssem.at[flow, j], recv_sem=rsem.at[flow, j],
             device_id=to, device_id_type=MESH,
@@ -120,8 +135,6 @@
             amp_hi[to, seg * CH : (seg + 1) * CH] = hi
             amp_lo[to, seg * CH : (seg + 1) * CH] = (a - hi.astype(f32)).astype(bf16)
         return carry
-
-    amplitude(0, 0)
 
     def whiten(m, carry):
         @pl.when(m < STEPS - 1)
@@ -146,15 +159,40 @@
         for b in range(SPAN // 16):
             block = [turned[pl.ds(b * 16 + t, 8, stride=SPAN), :] for t in range(16)]
             block = jnp.concatenate(block, axis=0).astype(bf16)
-            j = m * 2 + b // 4
-            white[0, j, (b % 4) * 2, s] = block[:64]
-            white[0, j, (b % 4) * 2 + 1, s] = block[64:]
-        for j in (m * 2, m * 2 + 1):
-            for flow in (OWN_X, NEAR, LEG1, OWN_SIB):
-                copy(flow, j).start()
-        return carry
-
-    lax.fori_loop(0, STEPS, whiten, 0)
+            j = m * SHARE + (2 * b) // GROUPS
+            white[0, j, s, (2 * b) % GROUPS] = block[:64]
+            white[0, j, s, (2 * b + 1) % GROUPS] = block[64:]
+        return carry
+
+    def send_own(j):
+        copy(OWN_X, j).start()
+        pl.when(sends_near)(lambda: copy(NEAR, j).start())
+        pl.when(sends_far)(lambda: copy(LEG1, j).start())
+
+    amplitude(0, 0)
+    whiten(0, 0)
+    pl.semaphore_wait(barrier, greeted)
+    for j in range(min(WINDOW, SHARE)):
+        send_own(j)
+    lax.fori_loop(1, STEPS, whiten, 0)
+    for j in range(SHARE, WINDOW):
+        send_own(j)
+
+    def to_sibling(j, carry):
+        copy(OWN_SIB, j).start()
+        return carry
+
+    lax.fori_loop(0, PIECES, to_sibling, 0)
+
+    def clear(d):
+        def one(j, carry):
+            white[d, j] = jnp.zeros(white.shape[2:], bf16)
+            return carry
+
+        lax.fori_loop(0, PIECES, one, 0)
+
+    pl.when(jnp.logical_not(gets_near))(lambda: clear(1))
+    pl.when(jnp.logical_not(gets_far))(lambda: clear(2))
 
     row = lax.broadcasted_iota(jnp.int32, (ROWS, CH), 0)
     col = lax.broadcasted_iota(jnp.int32, (ROWS, CH), 1)
@@ -163,8 +201,11 @@
     col = lax.broadcasted_iota(jnp.int32, (8, 256), 1)
     diag[...] = jnp.where(row == (col // 8) % 8, 1.0, 0.0)
 
+    def group(d, j, g):
+        return white[d, j, :, g].reshape(256, CH)
+
     def turn_rows(j, g):
-        re = dot_nt(pick[...], white[0, j, g].reshape(256, CH))
+        re = dot_nt(pick[...], group(0, j, g))
         col = lax.broadcasted_iota(jnp.int32, (ROWS, 256), 1)
         rows32[j * GROUPS + g, :ROWS] = re
         rows32[j * GROUPS + g, ROWS:] = jnp.where(col % 8 < 4, pltpu.roll(re, 252, 1), -pltpu.roll(re, 4, 1))
@@ -178,32 +219,28 @@
     def crosses(j, g, slots):
         both = []
         for u in (g, g + 1):
-            right = [white[d, j, u].reshape(256, CH) for d in slots]
+            right = [group(d, j, u) for d in slots]
             right = right[0] if len(right) == 1 else jnp.concatenate(right, axis=1)
             both.append(dot(left(j, u), right).reshape(2 * ROWS, 8, right.shape[1]))
         return jnp.concatenate(both, axis=1).astype(bf16)
 
-    def project(j, count, into, first):
+    def project(j, count, source, into, first):
         def some(q, carry):
             for u in range(8):
                 p = q * 8 + u
-                got = dot(table[j // 2], cross[p])
+                got = dot(table[j // SHARE], source[p])
                 into[p] = got if first else into[p] + got
             return carry
 
         lax.fori_loop(0, count // 8, some, 0)
 
-    def project_at(j, count, into):
-        @pl.when(j == 1)
-        def _():
-            project(j, count, into, True)
-
-        @pl.when((j % 2 == 1) & (j > 1))
-        def _():
-            project(j, count, into, False)
+    def project_at(j, count, source, into, pieces):
+        pl.when(j == SHARE - 1)(lambda: project(j, count, source, into, True))
+        later = (j % SHARE == SHARE - 1) & (j > SHARE - 1) & (j < pieces)
+        pl.when(later)(lambda: project(j, count, source, into, False))
 
     def bins_at(j, i, part):
-        return pl.ds(pl.multiple_of(part * SPAN + (j % 2) * 64 + i * 16, 16), 16)
+        return pl.ds(pl.multiple_of(part * SPAN + (j % SHARE) * (8 * GROUPS) + i * 16, 16), 16)
 
     def compute0(j):
         copy(OWN_SIB, j).wait_recv()
@@ -214,92 +251,126 @@
             got = crosses(j, 2 * i, (0,)).reshape(2, ROWS // 2, 2, 16, CH)
             for part in range(2):
                 for h in range(2):
-                    cross[pl.ds(0, ROWS // 2), bins_at(j, i, part), h * CH : (h + 1) * CH] = got[part, :, h]
-        project_at(j, ROWS // 2, acc0)
+                    cross0[:, bins_at(j, i, part), h * CH : (h + 1) * CH] = got[part, :, h]
+        project_at(j, ROWS // 2, cross0, acc0, PIECES)
 
     def compute12(j):
-        for flow in (NEAR_SIB, NEAR2_SIB, FAR_SIB, FAR2_SIB):
-            copy(flow, j).wait_recv()
+        @pl.when(gets_near)
+        def _():
+            copy(NEAR_SIB, j).wait_recv()
+            copy(NEAR2_SIB, j).wait_recv()
+
+        @pl.when(gets_far)
+        def _():
+            copy(FAR_SIB, j).wait_recv()
+            copy(FAR2_SIB, j).wait_recv()
+
         for i in range(GROUPS // 2):
             got = crosses(j, 2 * i, (1, 2)).reshape(2, ROWS, 16, 2 * CH)
             for part in range(2):
                 cross[:, bins_at(j, i, part), :] = got[part]
-        project_at(j, ROWS, acc)
-
-    def first_half(j, carry):
+        project_at(j, ROWS, cross, acc, PIECES - SHARE)
+
+    def own_arrived(j):
         copy(OWN_X, j).wait_recv()
-        copy(NEAR2, j).start()
+        pl.when(sends_near)(lambda: copy(NEAR2, j).start())
         copy(OWN2_SIB, j).start()
-        copy(LEG1, j).wait_recv()
-        copy(LEG2, j).start()
-        copy(NEAR, j).wait_recv()
-        copy(NEAR_SIB, j).start()
-
-        @pl.when(j > 0)
-        def _():
-            compute0(j - 1)
-
-        return carry
-
-    lax.fori_loop(0, PIECES, first_half, 0)
-    compute0(PIECES - 1)
+
+        @pl.when(relays)
+        def _():
+            copy(LEG1, j).wait_recv()
+            copy(LEG2, j).start()
+
+        @pl.when(gets_near)
+        def _():
+            copy(NEAR, j).wait_recv()
+            copy(NEAR_SIB, j).start()
+
+    def far_arrived(j):
+        @pl.when(gets_far)
+        def _():
+            copy(LEG2, j).wait_recv()
+            copy(FAR_X, j).start()
+            copy(FAR_SIB, j).start()
+
+        @pl.when(gets_near)
+        def _():
+            copy(NEAR2, j).wait_recv()
+            copy(NEAR2_SIB, j).start()
 
     def far_across(j):
-        copy(FAR_X, j).wait_recv()
-        copy(FAR2_SIB, j).start()
-
-    def second_half(j, carry):
-        copy(LEG2, j).wait_recv()
-        copy(FAR_X, j).start()
-        copy(FAR_SIB, j).start()
-        copy(NEAR2, j).wait_recv()
-        copy(NEAR2_SIB, j).start()
-
-        @pl.when(j > 0)
-        def _():
-            far_across(j - 1)
-
-        @pl.when(j > 1)
-        def _():
-            compute12(j - 2)
-
-        return carry
-
-    lax.fori_loop(0, PIECES, second_half, 0)
-    compute12(PIECES - 2)
-    far_across(PIECES - 1)
-    compute12(PIECES - 1)
+        @pl.when(gets_far)
+        def _():
+            copy(FAR_X, j).wait_recv()
+            copy(FAR2_SIB, j).start()
+
+    def step(t, carry):
+        pl.when(t + WINDOW < PIECES)(lambda: send_own(t + WINDOW))
+        pl.when(t < PIECES)(lambda: own_arrived(t))
+        pl.when((t >= 1) & (t < PIECES + 1))(lambda: compute0(t - 1))
+        pl.when((t >= LAG_FAR) & (t < PIECES + LAG_FAR))(lambda: far_arrived(t - LAG_FAR))
+        pl.when((t >= LAG_ACROSS) & (t < PIECES + LAG_ACROSS))(lambda: far_across(t - LAG_ACROSS))
+        pl.when(t >= LAG_LAST)(lambda: compute12(t - LAG_LAST))
+        return carry
+
+    lax.fori_loop(0, PIECES + LAG_LAST, step, 0)
 
     def sent(j, carry):
-        for flow in range(FLOWS):
+        for flow in (OWN_SIB, OWN_X, OWN2_SIB):
             copy(flow, j).wait_send()
+        for flow, present in (
+            (NEAR, sends_near), (NEAR2, sends_near), (LEG1, sends_far), (LEG2, relays),
+            (NEAR_SIB, gets_near),
+            (NEAR2_SIB, gets_near), (FAR_SIB, gets_far), (FAR_X, gets_far), (FAR2_SIB, gets_far),
+        ):
+            pl.when(present)(copy(flow, j).wait_send)
         return carry
 
     lax.fori_loop(0, PIECES, sent, 0)
 
 
-def finish(norm, band, acc0, acc, out):
+def finish(norm, band, table, acc0, acc, cross, out, stage, sem):
     c = lax.axis_index("chan")
     reach = jnp.minimum(band[c], BLOCKS - 1 - c)
-    p = pl.program_id(0)
-    for h in range(2):
-        out[h, 0] = (acc0[p, :, h * CH : (h + 1) * CH] * norm).T
-        for d in (1, 2):
-            live = jnp.full((CH, LAGS), reach, jnp.int32) >= d
-            out[h, d] = jnp.where(live, (acc[2 * p + h, :, (d - 1) * CH : d * CH] * norm).T, 0.0)
-
-
-def per_device(table, spectra, half_width, band):
+
+    def write(p):
+        return pltpu.make_async_copy(stage.at[pl.ds(2 * p, 2)], out.at[pl.ds(2 * p, 2)], sem.at[p])
+
+    def some(q, carry):
+        for p in [4 * q + u for u in range(4)]:
+            for h in range(2):
+                stage[2 * p + h, 0] = (acc0[p, :, h * CH : (h + 1) * CH] * norm).T
+                got = (acc[2 * p + h] + dot(table[...], cross[2 * p + h])) * norm
+                for d in (1, 2):
+                    live = jnp.full((CH, LAGS), reach, jnp.int32) >= d
+                    stage[2 * p + h, d] = jnp.where(live, got[:, (d - 1) * CH : d * CH].T, 0.0)
+            write(p).start()
+        return carry
+
+    lax.fori_loop(0, ROWS // 8, some, 0)
+
+    def written(p, carry):
+        write(p).wait()
+        return carry
+
+    lax.fori_loop(0, ROWS // 2, written, 0)
+
+
+def per_device(table, last, spectra, half_width, band):
     norm = 1.0 / math.sqrt(4 * spectra.shape[1] * BINS)
     vmem = pl.BlockSpec(memory_space=pltpu.VMEM)
     smem = pl.BlockSpec(memory_space=pltpu.SMEM)
-    acc0, acc = pl.pallas_call(
+    sums = pl.pallas_call(
         gather,
-        out_shape=[pltpu.VMEM((ROWS // 2, LAGS, 2 * CH), f32), pltpu.VMEM((ROWS, LAGS, 2 * CH), f32)],
+        out_shape=[
+            pltpu.VMEM((ROWS // 2, LAGS, 2 * CH), f32),
+            pltpu.VMEM((ROWS, LAGS, 2 * CH), f32),
+            pltpu.VMEM((ROWS, 2 * SPAN, 2 * CH), bf16),
+        ],
         in_specs=[vmem, vmem, vmem],
-        out_specs=[vmem, vmem],
+        out_specs=[vmem, vmem, vmem],
         scratch_shapes=[
-            pltpu.VMEM((3, PIECES, GROUPS, 4, 64, CH), bf16),
+            pltpu.VMEM((3, PIECES, 4, GROUPS, 64, CH), bf16),
             pltpu.VMEM((PIECES, GROUPS, 64, CH), bf16),
             pltpu.VMEM((BINS + SPAN, 4 * CH), bf16),
             pltpu.VMEM((BINS + SPAN, 4 * CH), bf16),
@@ -307,7 +378,7 @@
             pltpu.VMEM((ROWS, CH), bf16),
             pltpu.VMEM((8, 256), f32),
             pltpu.VMEM((PIECES * GROUPS, 2 * ROWS, 256), f32),
-            pltpu.VMEM((ROWS, 2 * SPAN, 2 * CH), bf16),
+            pltpu.VMEM((ROWS // 2, 2 * SPAN, 2 * CH), bf16),
             pltpu.SemaphoreType.DMA((FLOWS, PIECES)),
             pltpu.SemaphoreType.DMA((FLOWS, PIECES)),
         ],
@@ -315,25 +386,24 @@
         cost_estimate=pl.CostEstimate(flops=2 * 5_500_000_000, bytes_accessed=16_000_000, transcendentals=0),
         name="gather",
     )(spectra, half_width.reshape(STEPS, SPAN), table)
-    acc0 = pltpu.with_memory_space_constraint(acc0, pltpu.VMEM)
-    acc = pltpu.with_memory_space_constraint(acc, pltpu.VMEM)
+    sums = [pltpu.with_memory_space_constraint(x, pltpu.VMEM) for x in sums]
     return pl.pallas_call(
         partial(finish, norm),
-        grid=(ROWS // 2,),
         out_shape=jax.ShapeDtypeStruct((ROWS, 3, CH, LAGS), f32),
-        in_specs=[smem, vmem, vmem],
-        out_specs=pl.BlockSpec((2, 3, CH, LAGS), lambda p: (p, 0, 0, 0)),
-        compiler_params=pltpu.CompilerParams(vmem_limit_bytes=8 * 2**20),
-        cost_estimate=pl.CostEstimate(flops=0, bytes_accessed=12_600_000, transcendentals=0),
+        in_specs=[smem, vmem, vmem, vmem, vmem],
+        out_specs=pl.BlockSpec(memory_space=pl.ANY),
+        scratch_shapes=[pltpu.VMEM((ROWS, 3, CH, LAGS), f32), pltpu.SemaphoreType.DMA((ROWS // 2,))],
+        compiler_params=pltpu.CompilerParams(vmem_limit_bytes=VMEM_FINISH),
+        cost_estimate=pl.CostEstimate(flops=2 * 540_000_000, bytes_accessed=12_600_000, transcendentals=0),
         name="finish",
-    )(band, acc0, acc)
+    )(band, last, *sums)
 
 
 def solution(mesh):
     table = lag_table()
 
     def body(spectra, half_width, band):
-        return per_device(jnp.asarray(table), spectra, half_width, band)
+        return per_device(jnp.asarray(table), jnp.asarray(table[-1]), spectra, half_width, band)
 
     in_specs = (P(None, "seg", None, "chan"), P(), P())
     out_specs = P(("chan", "seg"), None, None, None)

time: 109 us -> 93.5 us (0.86); the launches traced: 109 us -> 92.3 us
  Pallas kernels: 109 us -> 92.2 us
    pallas_call x1, Pallas kernels: 99.1 us -> 86.4 us  [per_device(): pl.pallas_call(gather, out_shape=[pltpu.VMEM((ROWS // 2, LAGS, 2 * CH), f...]
    pallas_call x1, Pallas kernels: 10.1 us -> 5.83 us  [per_device(): pl.pallas_call(partial(finish, norm), out_shape=jax.ShapeDtypeStruct((ROW...]
where the time goes in v3:
time: 93.5 us; the launch traced here: 92.3 us
  Pallas kernels  92.2 us (99%)
    pallas_call x1, Pallas kernels, per_device(): pl.pallas_call(gather, out_shape=[pltpu.VMEM((ROWS // 2, LAGS, 2 * CH), f...  86.4 us
    pallas_call x1, Pallas kernels, per_device(): pl.pallas_call(partial(finish, norm), out_shape=jax.ShapeDtypeStruct((ROW...  5.83 us

profile of v3, /device:TPU:1, one launch (start us, length us, event | category | flops | bytes accessed | tf_op | source)
XLA Modules:
  0.0 92.3 jit_solution(5536801626317652451)
XLA Ops:
  0.0 0.0 copy-start
  0.0 0.0 copy-start.1
  0.0 86.4 %gather.1 = (f32[16,256,256]{2,1,0:T(8,128)S(1)}, f32[32,256,256]{2,1,0:T(8,128)S(1)}, bf16[32,256,256]{2,1,0:T(8,128)(2,1)S(1)}) custom-call(bf16[2,4,768,128]{3,2,1,0:T(8,128)(2,1)} %spec.1, s32[6,128]{1,0:T(8,128)} %bitcast.1, bf16[6,256,256]{2,1,0:T(8,128)(2,1)} %constant.4.clone.table), custom_call_target="tpu_custom_call" | custom-call | flops 11000000512 | bytes 16000000 | tf_op jit(solution)/shard_map/gather/pallas_call | solution.py:363
  86.4 0.0 copy-done
  86.4 0.0 copy-done.1
  86.4 5.8 %finish.1 = f32[32,3,128,256]{3,2,1,0:T(8,128)} custom-call(s32[32]{0:T(128)S(1)} %copy-done.1, bf16[256,256]{1,0:T(8,128)(2,1)S(1)} %copy-done, f32[16,256,256]{2,1,0:T(8,128)S(1)} %get-tuple-element.8.acc0, f32[32,256,256]{2,1,0:T(8,128)S(1)} %get-tuple-element.9.acc, bf16[32,256,256]{2,1,0:T(8,128)(2,1)S(1)} %get-tuple-element.10.cross), custom_call_target="tpu_custom_call" | custom-call | flops 1080000000 | bytes 12600000 | tf_op jit(solution)/shard_map/finish/pallas_call | solution.py:390
Async XLA Ops:
  0.0 86.4 %copy-start = (bf16[256,256]{1,0:T(8,128)(2,1)S(1)}, bf16[256,256]{1,0:T(8,128)(2,1)}, u32[]{:S(2)}) copy-start(bf16[256,256]{1,0:T(8,128)(2,1)} %constant.5.clone.table) | copy-start | bytes 393220
  0.0 86.4 %copy-start.1 = (s32[32]{0:T(128)S(1)}, s32[32]{0:T(128)}, u32[]{:S(2)}) copy-start(s32[32]{0:T(128)} %band.1) | copy-start | bytes 388

commit v4 on v3

--- a/solution.py
+++ b/solution.py
@@ -22,6 +22,7 @@
 PIECES = 12
 WINDOW = 3
 LAG_FAR, LAG_ACROSS, LAG_LAST = 2, 4, 5
+DOWN = (4,)
 GROUPS = BINS // 8 // PIECES
 SPAN = 128
 STEPS = BINS // SPAN
@@ -35,6 +36,7 @@
 
 (OWN_SIB, OWN_X, NEAR, LEG1, OWN2_SIB, NEAR2, NEAR_SIB, NEAR2_SIB, LEG2, FAR_SIB, FAR_X, FAR2_SIB) = range(12)
 FLOWS = 12
+DOWN2, NEAR_X = range(FLOWS, FLOWS + 2)
 
 
 def lag_table():
@@ -57,9 +59,18 @@
 
 
 def gather(
-    spec, half, table, acc0, acc, cross,
-    white, relay, amp_hi, amp_lo, turned, pick, diag, rows32, cross0, ssem, rsem,
+    spec_hbm, half, table_hbm, acc0, acc, cross,
+    spec, table, load_sem, white, relay, amp_hi, amp_lo, turned, pick, diag, rows32, cross0, ssem, rsem,
 ):
+    def load(m):
+        rows = pl.ds(m * SPAN, SPAN)
+        return pltpu.make_async_copy(spec_hbm.at[:, :, rows], spec.at[:, :, rows], load_sem.at[m])
+
+    load_table = pltpu.make_async_copy(table_hbm, table, load_sem.at[STEPS])
+    for m in range(STEPS):
+        load(m).start()
+    load_table.start()
+
     c = lax.axis_index("chan")
     s = lax.axis_index("seg")
     xl = s // 2
@@ -85,6 +96,7 @@
     sends_near, gets_near = c > 0, c < BLOCKS - 1
     sends_far, gets_far = c > 1, c < BLOCKS - 2
     relays = leg_from[0] > 1
+    passes_down = sends_near & gets_near
 
     barrier = pltpu.get_barrier_semaphore()
     greets = ((sib, None), (across, None), (near_to, sends_near), (near_from, gets_near), (leg_to, c != 1), (leg_from, c != BLOCKS - 2))
@@ -99,7 +111,7 @@
             greeted = greeted + present.astype(jnp.int32)
 
     def copy(flow, j):
-        here, there, to = {
+        here, there, to, *slot = {
             OWN_SIB: ((0, s), (0, s), sib),
             OWN_X: ((0, s), (0, s), across),
             NEAR: ((0, s), (1, s), near_to),
@@ -112,12 +124,27 @@
             FAR_SIB: ((2, fq), (2, fq), sib),
             FAR_X: ((2, fq), (2, fq), across),
             FAR2_SIB: ((2, fq2), (2, fq2), sib),
+            DOWN2: ((1, nq), (2, nq), near_to, LEG2),
+            NEAR_X: ((1, nq), (1, nq), across, NEAR2),
         }[flow]
+        slot = slot[0] if slot else flow
         place = lambda at: relay.at[j] if at is None else white.at[at[0], j, at[1]]
         return pltpu.make_async_remote_copy(
-            src_ref=place(here), dst_ref=place(there), send_sem=ssem.at[flow, j], recv_sem=rsem.at[flow, j],
+            src_ref=place(here), dst_ref=place(there), send_sem=ssem.at[slot, j], recv_sem=rsem.at[slot, j],
             device_id=to, device_id_type=MESH,
         )
+
+    def start(present, flow, j):
+        pl.when(present)(lambda: copy(flow, j).start())
+
+    def plain(j):
+        hit = j != DOWN[0]
+        for v in DOWN[1:]:
+            hit = hit & (j != v)
+        return jnp.asarray(hit)
+
+    def down(j):
+        return jnp.logical_not(plain(j))
 
     amp_hi[pl.ds(0, REACH), :] = jnp.zeros((REACH, 4 * CH), bf16)
     amp_lo[pl.ds(0, REACH), :] = jnp.zeros((REACH, 4 * CH), bf16)
@@ -125,6 +152,7 @@
     amp_lo[pl.ds(REACH + BINS, SPAN - REACH), :] = jnp.zeros((SPAN - REACH, 4 * CH), bf16)
 
     def amplitude(m, carry):
+        load(m).wait()
         rows = pl.ds(pl.multiple_of(m * SPAN, SPAN), SPAN)
         to = pl.ds(pl.multiple_of(m * SPAN + REACH, REACH), SPAN)
         for seg in range(4):
@@ -166,8 +194,8 @@
 
     def send_own(j):
         copy(OWN_X, j).start()
-        pl.when(sends_near)(lambda: copy(NEAR, j).start())
-        pl.when(sends_far)(lambda: copy(LEG1, j).start())
+        start(sends_near, NEAR, j)
+        start(sends_far & plain(j), LEG1, j)
 
     amplitude(0, 0)
     whiten(0, 0)
@@ -183,6 +211,7 @@
         return carry
 
     lax.fori_loop(0, PIECES, to_sibling, 0)
+    load_table.wait()
 
     def clear(d):
         def one(j, carry):
@@ -273,10 +302,10 @@
 
     def own_arrived(j):
         copy(OWN_X, j).wait_recv()
-        pl.when(sends_near)(lambda: copy(NEAR2, j).start())
+        start(sends_near & plain(j), NEAR2, j)
         copy(OWN2_SIB, j).start()
 
-        @pl.when(relays)
+        @pl.when(relays & plain(j))
         def _():
             copy(LEG1, j).wait_recv()
             copy(LEG2, j).start()
@@ -284,6 +313,8 @@
         @pl.when(gets_near)
         def _():
             copy(NEAR, j).wait_recv()
+            start(sends_near & down(j), DOWN2, j)
+            start(down(j), NEAR_X, j)
             copy(NEAR_SIB, j).start()
 
     def far_arrived(j):
@@ -303,6 +334,16 @@
         def _():
             copy(FAR_X, j).wait_recv()
             copy(FAR2_SIB, j).start()
+
+    def sent(j):
+        for flow in (OWN_SIB, OWN_X, OWN2_SIB):
+            copy(flow, j).wait_send()
+        for flow, present in (
+            (NEAR, sends_near), (NEAR_SIB, gets_near), (NEAR2_SIB, gets_near), (FAR_SIB, gets_far), (FAR_X, gets_far),
+            (FAR2_SIB, gets_far), (LEG1, sends_far & plain(j)), (LEG2, relays & plain(j)), (NEAR2, sends_near & plain(j)),
+            (DOWN2, passes_down & down(j)), (NEAR_X, gets_near & down(j)),
+        ):
+            pl.when(present)(copy(flow, j).wait_send)
 
     def step(t, carry):
         pl.when(t + WINDOW < PIECES)(lambda: send_own(t + WINDOW))
@@ -311,30 +352,18 @@
         pl.when((t >= LAG_FAR) & (t < PIECES + LAG_FAR))(lambda: far_arrived(t - LAG_FAR))
         pl.when((t >= LAG_ACROSS) & (t < PIECES + LAG_ACROSS))(lambda: far_across(t - LAG_ACROSS))
         pl.when(t >= LAG_LAST)(lambda: compute12(t - LAG_LAST))
+        pl.when(t >= LAG_LAST)(lambda: sent(t - LAG_LAST))
         return carry
 
     lax.fori_loop(0, PIECES + LAG_LAST, step, 0)
-
-    def sent(j, carry):
-        for flow in (OWN_SIB, OWN_X, OWN2_SIB):
-            copy(flow, j).wait_send()
-        for flow, present in (
-            (NEAR, sends_near), (NEAR2, sends_near), (LEG1, sends_far), (LEG2, relays),
-            (NEAR_SIB, gets_near),
-            (NEAR2_SIB, gets_near), (FAR_SIB, gets_far), (FAR_X, gets_far), (FAR2_SIB, gets_far),
-        ):
-            pl.when(present)(copy(flow, j).wait_send)
-        return carry
-
-    lax.fori_loop(0, PIECES, sent, 0)
 
 
 def finish(norm, band, table, acc0, acc, cross, out, stage, sem):
     c = lax.axis_index("chan")
     reach = jnp.minimum(band[c], BLOCKS - 1 - c)
 
-    def write(p):
-        return pltpu.make_async_copy(stage.at[pl.ds(2 * p, 2)], out.at[pl.ds(2 * p, 2)], sem.at[p])
+    def write(a):
+        return pltpu.make_async_copy(stage.at[a], out.at[a], sem.at[a])
 
     def some(q, carry):
         for p in [4 * q + u for u in range(4)]:
@@ -344,16 +373,16 @@
                 for d in (1, 2):
                     live = jnp.full((CH, LAGS), reach, jnp.int32) >= d
                     stage[2 * p + h, d] = jnp.where(live, got[:, (d - 1) * CH : d * CH].T, 0.0)
-            write(p).start()
+                write(2 * p + h).start()
         return carry
 
     lax.fori_loop(0, ROWS // 8, some, 0)
 
-    def written(p, carry):
-        write(p).wait()
-        return carry
-
-    lax.fori_loop(0, ROWS // 2, written, 0)
+    def written(a, carry):
+        write(a).wait()
+        return carry
+
+    lax.fori_loop(0, ROWS, written, 0)
 
 
 def per_device(table, last, spectra, half_width, band):
@@ -367,9 +396,12 @@
             pltpu.VMEM((ROWS, LAGS, 2 * CH), f32),
             pltpu.VMEM((ROWS, 2 * SPAN, 2 * CH), bf16),
         ],
-        in_specs=[vmem, vmem, vmem],
+        in_specs=[pl.BlockSpec(memory_space=pl.ANY), vmem, pl.BlockSpec(memory_space=pl.ANY)],
         out_specs=[vmem, vmem, vmem],
         scratch_shapes=[
+            pltpu.VMEM(spectra.shape, bf16),
+            pltpu.VMEM(table.shape, bf16),
+            pltpu.SemaphoreType.DMA((STEPS + 1,)),
             pltpu.VMEM((3, PIECES, 4, GROUPS, 64, CH), bf16),
             pltpu.VMEM((PIECES, GROUPS, 64, CH), bf16),
             pltpu.VMEM((BINS + SPAN, 4 * CH), bf16),
@@ -392,7 +424,7 @@
         out_shape=jax.ShapeDtypeStruct((ROWS, 3, CH, LAGS), f32),
         in_specs=[smem, vmem, vmem, vmem, vmem],
         out_specs=pl.BlockSpec(memory_space=pl.ANY),
-        scratch_shapes=[pltpu.VMEM((ROWS, 3, CH, LAGS), f32), pltpu.SemaphoreType.DMA((ROWS // 2,))],
+        scratch_shapes=[pltpu.VMEM((ROWS, 3, CH, LAGS), f32), pltpu.SemaphoreType.DMA((ROWS,))],
         compiler_params=pltpu.CompilerParams(vmem_limit_bytes=VMEM_FINISH),
         cost_estimate=pl.CostEstimate(flops=2 * 540_000_000, bytes_accessed=12_600_000, transcendentals=0),
         name="finish",

time: 93.5 us -> 92.4 us (0.988)
  the two profiles are of different devices: /device:TPU:1 before, /device:TPU:123 now
where the time goes in v4:
time: 92.4 us; the launch traced here: 92.3 us
  Pallas kernels  92.3 us (100%)
    pallas_call x1, Pallas kernels, per_device(): pl.pallas_call(gather, out_shape=[pltpu.VMEM((ROWS // 2, LAGS, 2 * CH), f...  86.3 us
    pallas_call x1, Pallas kernels, per_device(): pl.pallas_call(partial(finish, norm), out_shape=jax.ShapeDtypeStruct((ROW...  5.95 us

profile of v4, /device:TPU:123, one launch (start us, length us, event | category | flops | bytes accessed | tf_op | source)
XLA Modules:
  0.0 92.3 jit_solution(18000776378497893458)
XLA Ops:
  0.0 0.0 copy-start
  0.0 0.0 copy-start.1
  0.0 86.3 %gather.1 = (f32[16,256,256]{2,1,0:T(8,128)S(1)}, f32[32,256,256]{2,1,0:T(8,128)S(1)}, bf16[32,256,256]{2,1,0:T(8,128)(2,1)S(1)}) custom-call(bf16[2,4,768,128]{3,2,1,0:T(8,128)(2,1)} %spec_hbm.1, s32[6,128]{1,0:T(8,128)} %bitcast.1, bf16[6,256,256]{2,1,0:T(8,128)(2,1)} %constant.4.clone.table_hbm), custom_call_target="tpu_custom_call" | custom-call | flops 11000000512 | bytes 16000000 | tf_op jit(solution)/shard_map/gather/pallas_call | solution.py:392
  86.3 0.0 copy-done
  86.3 0.0 copy-done.1
  86.3 6.0 %finish.1 = f32[32,3,128,256]{3,2,1,0:T(8,128)} custom-call(s32[32]{0:T(128)S(1)} %copy-done.1, bf16[256,256]{1,0:T(8,128)(2,1)S(1)} %copy-done, f32[16,256,256]{2,1,0:T(8,128)S(1)} %get-tuple-element.8.acc0, f32[32,256,256]{2,1,0:T(8,128)S(1)} %get-tuple-element.9.acc, bf16[32,256,256]{2,1,0:T(8,128)(2,1)S(1)} %get-tuple-element.10.cross), custom_call_target="tpu_custom_call" | custom-call | flops 1080000000 | bytes 12600000 | tf_op jit(solution)/shard_map/finish/pallas_call | solution.py:422
Async XLA Ops:
  0.0 86.3 %copy-start = (bf16[256,256]{1,0:T(8,128)(2,1)S(1)}, bf16[256,256]{1,0:T(8,128)(2,1)}, u32[]{:S(2)}) copy-start(bf16[256,256]{1,0:T(8,128)(2,1)} %constant.5.clone.table) | copy-start | bytes 393220
  0.0 86.3 %copy-start.1 = (s32[32]{0:T(128)S(1)}, s32[32]{0:T(128)}, u32[]{:S(2)}) copy-start(s32[32]{0:T(128)} %band.1) | copy-start | bytes 388

commit v5 on v4

--- a/solution.py
+++ b/solution.py
@@ -20,7 +20,7 @@
 FLOOR = 0.2
 
 PIECES = 12
-WINDOW = 3
+WINDOW = 4
 LAG_FAR, LAG_ACROSS, LAG_LAST = 2, 4, 5
 DOWN = (4,)
 GROUPS = BINS // 8 // PIECES
@@ -206,11 +206,6 @@
     for j in range(SHARE, WINDOW):
         send_own(j)
 
-    def to_sibling(j, carry):
-        copy(OWN_SIB, j).start()
-        return carry
-
-    lax.fori_loop(0, PIECES, to_sibling, 0)
     load_table.wait()
 
     def clear(d):
@@ -303,6 +298,7 @@
     def own_arrived(j):
         copy(OWN_X, j).wait_recv()
         start(sends_near & plain(j), NEAR2, j)
+        copy(OWN_SIB, j).start()
         copy(OWN2_SIB, j).start()
 
         @pl.when(relays & plain(j))

time: 92.4 us -> 92.6 us (level)
  no operation moved by 1% of the time
where the time goes in v5:
time: 92.6 us; the launch traced here: 92.5 us
  Pallas kernels  92.4 us (100%)
    pallas_call x1, Pallas kernels, per_device(): pl.pallas_call(gather, out_shape=[pltpu.VMEM((ROWS // 2, LAGS, 2 * CH), f...  86.5 us
    pallas_call x1, Pallas kernels, per_device(): pl.pallas_call(partial(finish, norm), out_shape=jax.ShapeDtypeStruct((ROW...  5.95 us

profile of v5, /device:TPU:123, one launch (start us, length us, event | category | flops | bytes accessed | tf_op | source)
XLA Modules:
  0.0 92.5 jit_solution(13274707287064701233)
XLA Ops:
  0.0 0.0 copy-start
  0.0 0.0 copy-start.1
  0.0 86.5 %gather.1 = (f32[16,256,256]{2,1,0:T(8,128)S(1)}, f32[32,256,256]{2,1,0:T(8,128)S(1)}, bf16[32,256,256]{2,1,0:T(8,128)(2,1)S(1)}) custom-call(bf16[2,4,768,128]{3,2,1,0:T(8,128)(2,1)} %spec_hbm.1, s32[6,128]{1,0:T(8,128)} %bitcast.1, bf16[6,256,256]{2,1,0:T(8,128)(2,1)} %constant.4.clone.table_hbm), custom_call_target="tpu_custom_call" | custom-call | flops 11000000512 | bytes 16000000 | tf_op jit(solution)/shard_map/gather/pallas_call | solution.py:388
  86.5 0.0 copy-done
  86.5 0.0 copy-done.1
  86.5 5.9 %finish.1 = f32[32,3,128,256]{3,2,1,0:T(8,128)} custom-call(s32[32]{0:T(128)S(1)} %copy-done.1, bf16[256,256]{1,0:T(8,128)(2,1)S(1)} %copy-done, f32[16,256,256]{2,1,0:T(8,128)S(1)} %get-tuple-element.8.acc0, f32[32,256,256]{2,1,0:T(8,128)S(1)} %get-tuple-element.9.acc, bf16[32,256,256]{2,1,0:T(8,128)(2,1)S(1)} %get-tuple-element.10.cross), custom_call_target="tpu_custom_call" | custom-call | flops 1080000000 | bytes 12600000 | tf_op jit(solution)/shard_map/finish/pallas_call | solution.py:418
Async XLA Ops:
  0.0 86.5 %copy-start = (bf16[256,256]{1,0:T(8,128)(2,1)S(1)}, bf16[256,256]{1,0:T(8,128)(2,1)}, u32[]{:S(2)}) copy-start(bf16[256,256]{1,0:T(8,128)(2,1)} %constant.5.clone.table) | copy-start | bytes 393220
  0.0 86.5 %copy-start.1 = (s32[32]{0:T(128)S(1)}, s32[32]{0:T(128)}, u32[]{:S(2)}) copy-start(s32[32]{0:T(128)} %band.1) | copy-start | bytes 388
